TPU v7x, 512 devices: a whole 4x8x8 slice. The times are simulated.
512 devices in a mesh: dp: 16 (over x, z_lo, core), ctx: 32 (over z_hi, y).
Axes of the slice: x: 4, y: 8, z: 8 (z_hi: 4, z_lo: 2; z = z_hi * 2 + z_lo), core: 2. Of those that a mesh axis runs over, the one named last changes fastest.
Arguments:
- queries: bfloat16 [16, 4096, 1024], P('dp', 'ctx'), may hold values from -60 to 60
- keys: bfloat16 [16, 4096, 128], P('dp', 'ctx'), may hold values from -6 to 6
- values: bfloat16 [16, 4096, 192], P('dp', 'ctx'), may hold values from -96 to 96
- features_fine: bfloat16 [16, 8192, 1536], P('dp', 'ctx'), may hold values from -6 to 6
- rc_state: bfloat16 [16, 4096, 1536], P('dp', 'ctx'), may hold values from -6 to 6
- conv_weight: float32 [5, 1536], replicated, may hold values from -2.5 to 2.5
Outputs:
- d_fine: bfloat16 [16, 8192, 1536], P('dp', 'ctx')
- d_weight: float32 [5, 1536], replicated
All inputs are finite; a program needn't handle non-finite values.
Results may differ from a plain program's by a relative error of at most 0.0085.
Values may be sent and summed in bfloat16 or wider, within the bound.
A program may use at most 64 MiB of HBM per device.

v0:
```python
import math
import jax
import jax.numpy as jnp
from jax import lax
from jax.sharding import PartitionSpec as P

HEADS = 8
KW = 5


def padded_2(cells, sides, width):
    for axis, dim in sides:
        count = lax.axis_size(axis)
        ends = count - 1
        head = lax.slice_in_dim(cells, 0, width, axis=dim)
        tail = lax.slice_in_dim(cells, cells.shape[dim] - width, cells.shape[dim], axis=dim)
        cells = jnp.concatenate(
            [
                lax.ppermute(tail, axis, [(i, (i + 1) % count) for i in range(ends)]),
                cells,
                lax.ppermute(head, axis, [((i + 1) % count, i) for i in range(ends)]),
            ],
            axis=dim,
        )
    return cells


def body(queries, keys, values, features_fine, rc_state, conv_weight):
    tok_rows = queries.shape[1]
    key_size = keys.shape[2]
    value_size = values.shape[2]
    q_heads = queries[0].reshape(tok_rows, HEADS, key_size)
    ctx_count = lax.axis_size("ctx")
    run_top = jnp.full((tok_rows, HEADS), -1e30, jnp.float32)
    key_piece = lax.all_gather(keys, "ctx", axis=1, tiled=True)
    value_piece = lax.all_gather(values, "ctx", axis=1, tiled=True)
    scores = jnp.einsum(
        "qhd,kd->qhk", q_heads, key_piece[0], preferred_element_type=jnp.float32
    ) * key_size ** (-0.5)
    new_top = jnp.maximum(run_top, jnp.max(scores, axis=-1))
    expd = jnp.exp(scores - new_top[..., None])
    new_total = jnp.sum(expd, axis=-1)
    mixed = jnp.einsum(
        "qhk,kv->qhv", expd.astype(jnp.bfloat16), value_piece[0], preferred_element_type=jnp.float32
    )
    attended = (mixed / new_total[..., None]).reshape(tok_rows, HEADS * value_size)[None]
    padded = padded_2(features_fine, (("ctx", 1),), 2)
    taps = [padded[:, k : k + 2 * tok_rows : 2, :].astype(jnp.float32) for k in range(KW)]
    coarse = conv_weight[0] * taps[0]
    for k in range(1, KW):
        coarse = coarse + conv_weight[k] * taps[k]
    slices = lax.all_to_all(rc_state, "ctx", split_axis=2, concat_axis=0, tiled=True)
    flipped = slices[::-1]
    mirrored = lax.all_to_all(flipped, "ctx", split_axis=0, concat_axis=2, tiled=True)
    grad = coarse + attended - mirrored[:, ::-1, :].astype(jnp.float32)
    gpad = padded_2(grad.astype(jnp.bfloat16), (("ctx", 1),), 1).astype(grad.dtype)
    even = (
        conv_weight[0] * gpad[:, 2:]
        + conv_weight[2] * gpad[:, 1:-1]
        + conv_weight[4] * gpad[:, :-2]
    )
    odd = conv_weight[1] * gpad[:, 2:] + conv_weight[3] * gpad[:, 1:-1]
    d_fine = (
        jnp.stack([even, odd], axis=2)
        .reshape(grad.shape[0], 2 * tok_rows, grad.shape[2])
        .astype(jnp.bfloat16)
    )
    partial_grad = jnp.stack([jnp.sum(grad * taps[k], axis=(0, 1)) for k in range(KW)])
    summed = lax.psum(partial_grad, ("dp", "ctx"))
    scale = 1.0 / math.sqrt(lax.axis_size("dp") * tok_rows * ctx_count)
    return (d_fine, summed * scale)


def solution(mesh):
    placed = (
        P("dp", "ctx", None),
        P("dp", "ctx", None),
        P("dp", "ctx", None),
        P("dp", "ctx", None),
        P("dp", "ctx", None),
        P(),
    )
    return jax.shard_map(
        body, mesh=mesh, in_specs=placed, out_specs=(P("dp", "ctx", None), P()), check_vma=False
    )
```

profile of v0, /device:TPU:184, one launch (start us, length us, event | category | flops | bytes accessed | tf_op | source)
XLA Modules:
  0.0 341.5 jit_solution(18383458230890813925)
XLA Ops:
  7.2 0.0 all-gather.3.cloned.1.call-start
  7.2 0.7 all-gather.3.cloned.1.call-update
  7.9 2.2 copy.29
  10.1 0.5 broadcast.15
  10.6 8.8 %reduce.10 = bf16[1536,128]{1,0:T(8,128)(2,1)S(1)} reduce(bf16[1536,1,128]{2,1,0:T(2,128)(2,1)S(1)} %bitcast.34, bf16[]{:T(256)} %broadcast.15), dimensions={1}, to_apply=%bitcast.29.reduce_sub_computation | reduce | bytes 786434
  19.4 0.8 reshape.84
  20.2 13.8 %all-to-all-start = ((bf16[32,2,3072]{2,1,0:T(2,128)(2,1)}), bf16[32,2,3072]{2,1,0:T(2,128)(2,1)S(1)}, u32[]{:S(2)}, u32[]{:S(2)}) async-start(bf16[32,2,3072]{2,1,0:T(2,128)(2,1)} %reshape.84), calls=%async_computation | async-start | bytes 786432 | tf_op jit(solution)/shard_map/all_to_all | solution.py:52
  34.0 0.0 all-gather.5.cloned.1.call-start
  34.1 0.7 all-gather.5.cloned.1.call-update
  34.8 12.8 %all-to-all-done = bf16[32,2,3072]{2,1,0:T(2,128)(2,1)S(1)} async-done(((bf16[32,2,3072]{2,1,0:T(2,128)(2,1)}), bf16[32,2,3072]{2,1,0:T(2,128)(2,1)S(1)}, u32[]{:S(2)}, u32[]{:S(2)}) %all-to-all-start) | async-done | bytes 393248 | tf_op jit(solution)/shard_map/all_to_all | solution.py:52
  47.6 0.3 reshape.85
  47.9 0.1 copy.31
  48.0 0.8 rev.6
  48.7 8.5 %all-to-all-start.1 = ((bf16[32,128,48]{1,2,0:T(8,128)(2,1)}), bf16[32,128,48]{1,2,0:T(8,128)(2,1)S(1)}, u32[]{:S(2)}, u32[]{:S(2)}) async-start(bf16[32,128,48]{1,2,0:T(8,128)(2,1)} %rev.6), calls=%async_computation.1 | async-start | bytes 786432 | tf_op jit(solution)/shard_map/all_to_all | solution.py:54
  57.3 0.3 copy.24
  57.5 5.5 %collective-permute-start = (bf16[1,2,1536]{1,2,0:T(8,128)(2,1)S(1)}, bf16[1,2,1536]{1,2,0:T(8,128)(2,1)}, u32[]{:S(2)}, u32[]{:S(2)}) collective-permute-start(bf16[1,2,1536]{1,2,0:T(8,128)(2,1)S(1)} %copy.24), channel_id=1, source_target_pairs={{0,1},{1,2},{2,3},{3,4},{4,5},{5,6},{6,7},{7,8},{8,9},{9,10},{10,1... | collective-permute-start | bytes 18440 | tf_op jit(solution)/shard_map/ppermute | solution.py:19
  63.0 0.3 copy.25
  63.3 2.1 collective-permute-start.1
  65.4 0.1 slice_reduce_fusion.4
  65.5 0.3 copy.26
  65.8 1.0 copy.32
  66.8 14.4 %slice.65 = bf16[1,128,1536]{1,2,0:T(8,128)(2,1)S(1)} slice(bf16[1,256,1536]{1,2,0:T(8,128)(2,1)S(1)} %copy.26), slice={[0:1:1], [0:256:2], [0:1536:1]} | slice | bytes 786432 | tf_op jit(solution)/shard_map/slice | solution.py:48
  81.2 5.9 %collective-permute-done.1 = bf16[1,2,1536]{1,2,0:T(8,128)(2,1)} collective-permute-done((bf16[1,2,1536]{1,2,0:T(8,128)(2,1)S(1)}, bf16[1,2,1536]{1,2,0:T(8,128)(2,1)}, u32[]{:S(2)}, u32[]{:S(2)}) %collective-permute-start.1) | collective-permute-done | bytes 6176 | tf_op jit(solution)/shard_map/ppermute | solution.py:21
  87.1 1.8 pad_maximum_fusion
  88.9 14.4 %slice.61 = bf16[1,128,1536]{1,2,0:T(8,128)(2,1)S(1)} slice(bf16[1,260,1536]{1,2,0:T(8,128)(2,1)S(1)} %pad_maximum_fusion), slice={[0:1:1], [0:256:2], [0:1536:1]} | slice | bytes 786432 | tf_op jit(solution)/shard_map/slice | solution.py:48
  103.3 14.4 %slice.63 = bf16[1,128,1536]{1,2,0:T(8,128)(2,1)S(1)} slice(bf16[1,260,1536]{1,2,0:T(8,128)(2,1)S(1)} %pad_maximum_fusion), slice={[0:1:1], [1:257:2], [0:1536:1]} | slice | bytes 786432 | tf_op jit(solution)/shard_map/slice | solution.py:48
  117.7 14.7 %slice.67 = bf16[1,128,1536]{1,2,0:T(8,128)(2,1)S(1)} slice(bf16[1,260,1536]{1,2,0:T(8,128)(2,1)S(1)} %pad_maximum_fusion), slice={[0:1:1], [3:259:2], [0:1536:1]} | slice | bytes 786432 | tf_op jit(solution)/shard_map/slice | solution.py:48
  132.4 15.0 %slice.69 = bf16[1,128,1536]{1,2,0:T(8,128)(2,1)} slice(bf16[1,260,1536]{1,2,0:T(8,128)(2,1)S(1)} %pad_maximum_fusion), slice={[0:1:1], [4:260:2], [0:1536:1]} | slice | bytes 786432 | tf_op jit(solution)/shard_map/slice | solution.py:48
  147.4 1.3 rev.7
  148.7 0.0 all-gather.3.cloned.1.call-done
  148.8 9.3 %multiply_reduce_fusion = (f32[128,8]{0,1:T(8,128)S(1)}, f32[128,8,4096]{2,0,1:T(8,128)}) fusion(bf16[1,4096,128]{2,1,0:T(8,128)(2,1)} %all-gather.3.cloned.1.call-done, bf16[128,8,128]{2,1,0:T(8,128)(2,1)S(1)} %bitcast.36), kind=kOutput, calls=%fused_computation.1 | convolution fusion | flops 1082129408 | bytes 18092032 | tf_op jit(solution)/shard_map/qhd,kd->qhk/dot_general | solution.py:37
  158.0 8.6 %fusion = f32[128,8]{0,1:T(8,128)S(1)} fusion(f32[128,8,4096]{2,0,1:T(8,128)} %get-tuple-element.20, f32[128,8]{0,1:T(8,128)S(1)} %broadcast_maximum_fusion), kind=kLoop, calls=%fused_computation.2 | loop fusion | flops 12581888 | bytes 16785408 | tf_op jit(solution)/shard_map/reduce_sum | solution.py:42
  166.7 29.0 %all-gather.5.cloned.1.call-done = bf16[1,4096,192]{1,2,0:T(8,128)(2,1)} async-done(((bf16[1,128,192]{1,2,0:T(8,128)(2,1)}), bf16[1,4096,192]{1,2,0:T(8,128)(2,1)}) %all-gather.5.cloned.1.call-update) | async-done | bytes 1572880 | tf_op jit(solution)/shard_map/all_gather | solution.py:36
  195.6 8.0 %fusion.7 = f32[128,8,192]{0,2,1:T(8,128)S(1)} fusion(bf16[1,4096,192]{1,2,0:T(8,128)(2,1)} %all-gather.5.cloned.1.call-done, f32[128,8,4096]{2,0,1:T(8,128)} %get-tuple-element.20, f32[128,8]{0,1:T(8,128)S(1)} %broadcast_maximum_fusion, f32[128,8]{0,1:T(8,128)S(1)} %fusion), kind=kOutput, calls=%fused_computation.19 | convolution fusion | flops 1623392256 | bytes 19144704 | tf_op jit(solution)/shard_map/qhk,kv->qhv/dot_general | solution.py:43
  203.6 2.7 fusion.22
  206.4 0.1 stack.38
  206.5 93.2 %psum.7 = f32[5,1536]{1,0:T(8,128)S(1)} all-reduce(f32[5,1536]{1,0:T(8,128)S(1)} %stack.38), channel_id=1, replica_groups=mesh['dp'=16,'ctx'=32] {'dp','ctx'}, use_global_device_ids=true, to_apply=%region_7.0 | all-reduce | flops 7680 | bytes 61440 | tf_op jit(solution)/shard_map/psum | solution.py:69
  299.7 0.2 fusion.31
  299.9 6.2 %collective-permute-start.2 = (bf16[1,1,1536]{1,2,0:T(8,128)(2,1)S(1)}, bf16[1,1,1536]{1,2,0:T(8,128)(2,1)S(1)}, u32[]{:S(2)}, u32[]{:S(2)}) collective-permute-start(bf16[1,1,1536]{1,2,0:T(8,128)(2,1)S(1)} %get-tuple-element.17), channel_id=1, source_target_pairs={{0,1},{1,2},{2,3},{3,4},{4,5},{5,6},{6,7},{7,8},{8,9},{9,10},{10,1... | collective-permute-start | bytes 9224 | tf_op jit(solution)/shard_map/ppermute | solution.py:19
  306.1 1.9 collective-permute-start.3
  308.0 0.6 broadcast_multiply_fusion
  308.6 11.6 %collective-permute-done.2 = bf16[1,1,1536]{1,2,0:T(8,128)(2,1)S(1)} collective-permute-done((bf16[1,1,1536]{1,2,0:T(8,128)(2,1)S(1)}, bf16[1,1,1536]{1,2,0:T(8,128)(2,1)S(1)}, u32[]{:S(2)}, u32[]{:S(2)}) %collective-permute-start.2) | collective-permute-done | bytes 3104 | tf_op jit(solution)/shard_map/ppermute | solution.py:19
  320.2 10.3 %collective-permute-done.3 = bf16[1,1,1536]{1,2,0:T(8,128)(2,1)S(1)} collective-permute-done((bf16[1,1,1536]{1,2,0:T(8,128)(2,1)S(1)}, bf16[1,1,1536]{1,2,0:T(8,128)(2,1)S(1)}, u32[]{:S(2)}, u32[]{:S(2)}) %collective-permute-start.3) | collective-permute-done | bytes 3104 | tf_op jit(solution)/shard_map/ppermute | solution.py:21
  330.5 0.4 maximum_convert_fusion
  330.9 1.7 fusion.26
  332.6 0.1 pad_maximum_fusion.1
  332.7 0.8 copy.30
  333.5 1.2 convert_element_type.56
  (15 shorter events, 0.1 us)
Async XLA Ops:
  7.2 141.6 %all-gather.3.cloned.1.call-start = ((), (), s32[]{:S(2)}) async-start(), calls=%async_computation.2 | async-start | bytes 1081344 | tf_op jit(solution)/shard_map/all_gather | solution.py:35
  20.2 37.0 %copy-start.1 = (bf16[1,256,1536]{2,1,0:T(8,128)(2,1)S(1)}, bf16[1,256,1536]{2,1,0:T(8,128)(2,1)}, u32[]{:S(2)}) copy-start(bf16[1,256,1536]{2,1,0:T(8,128)(2,1)} %param.9) | copy-start | bytes 2359300
  20.2 27.4 %all-to-all-start = ((bf16[32,2,3072]{2,1,0:T(2,128)(2,1)}), bf16[32,2,3072]{2,1,0:T(2,128)(2,1)S(1)}, u32[]{:S(2)}, u32[]{:S(2)}) async-start(bf16[32,2,3072]{2,1,0:T(2,128)(2,1)} %reshape.84), calls=%async_computation | async-start | bytes 786432 | tf_op jit(solution)/shard_map/all_to_all | solution.py:52
  34.0 161.6 %all-gather.5.cloned.1.call-start = ((), (), s32[]{:S(2)}) async-start(), calls=%async_computation.3 | async-start | bytes 1622016 | tf_op jit(solution)/shard_map/all_gather | solution.py:36
  34.8 30.6 %copy-start.2 = (f32[5,1536]{1,0:T(8,128)S(1)}, f32[5,1536]{1,0:T(8,128)}, u32[]{:S(2)}) copy-start(f32[5,1536]{1,0:T(8,128)} %param.11) | copy-start | bytes 92164
  48.7 98.6 %all-to-all-start.1 = ((bf16[32,128,48]{1,2,0:T(8,128)(2,1)}), bf16[32,128,48]{1,2,0:T(8,128)(2,1)S(1)}, u32[]{:S(2)}, u32[]{:S(2)}) async-start(bf16[32,128,48]{1,2,0:T(8,128)(2,1)} %rev.6), calls=%async_computation.1 | async-start | bytes 786432 | tf_op jit(solution)/shard_map/all_to_all | solution.py:54
  57.5 23.6 %collective-permute-start = (bf16[1,2,1536]{1,2,0:T(8,128)(2,1)S(1)}, bf16[1,2,1536]{1,2,0:T(8,128)(2,1)}, u32[]{:S(2)}, u32[]{:S(2)}) collective-permute-start(bf16[1,2,1536]{1,2,0:T(8,128)(2,1)S(1)} %copy.24), channel_id=1, source_target_pairs={{0,1},{1,2},{2,3},{3,4},{4,5},{5,6},{6,7},{7,8},{8,9},{9,10},{10,1... | collective-permute-start | bytes 18440 | tf_op jit(solution)/shard_map/ppermute | solution.py:19
  63.3 23.8 %collective-permute-start.1 = (bf16[1,2,1536]{1,2,0:T(8,128)(2,1)S(1)}, bf16[1,2,1536]{1,2,0:T(8,128)(2,1)}, u32[]{:S(2)}, u32[]{:S(2)}) collective-permute-start(bf16[1,2,1536]{1,2,0:T(8,128)(2,1)S(1)} %copy.25), channel_id=1, source_target_pairs={{1,0},{2,1},{3,2},{4,3},{5,4},{6,5},{7,6},{8,7},{9,8},{10,9},{11,1... | collective-permute-start | bytes 18440 | tf_op jit(solution)/shard_map/ppermute | solution.py:21
  166.7 36.9 %copy-start = (bf16[1,128,1536]{1,2,0:T(8,128)(2,1)S(1)}, bf16[1,128,1536]{1,2,0:T(8,128)(2,1)}, u32[]{:S(2)}) copy-start(bf16[1,128,1536]{1,2,0:T(8,128)(2,1)} %slice.69) | copy-start | bytes 1179652
  299.9 20.3 %collective-permute-start.2 = (bf16[1,1,1536]{1,2,0:T(8,128)(2,1)S(1)}, bf16[1,1,1536]{1,2,0:T(8,128)(2,1)S(1)}, u32[]{:S(2)}, u32[]{:S(2)}) collective-permute-start(bf16[1,1,1536]{1,2,0:T(8,128)(2,1)S(1)} %get-tuple-element.17), channel_id=1, source_target_pairs={{0,1},{1,2},{2,3},{3,4},{4,5},{5,6},{6,7},{7,8},{8,9},{9,10},{10,1... | collective-permute-start | bytes 9224 | tf_op jit(solution)/shard_map/ppermute | solution.py:19
  306.1 24.4 %collective-permute-start.3 = (bf16[1,1,1536]{1,2,0:T(8,128)(2,1)S(1)}, bf16[1,1,1536]{1,2,0:T(8,128)(2,1)S(1)}, u32[]{:S(2)}, u32[]{:S(2)}) collective-permute-start(bf16[1,1,1536]{1,2,0:T(8,128)(2,1)S(1)} %get-tuple-element.18), channel_id=1, source_target_pairs={{1,0},{2,1},{3,2},{4,3},{5,4},{6,5},{7,6},{8,7},{9,8},{10,9},{11,1... | collective-permute-start | bytes 9224 | tf_op jit(solution)/shard_map/ppermute | solution.py:21
Sparse Core Ops, SparseCore 0:
  11.2 102.2 all-gather.2
  116.5 79.0 all-gather.4
where the time goes:
time: 342 us; the launch traced here: 341 us
  blocking collectives  93.2 us (27%)
  local copies, waits for them, and re-layouts  82.9 us (24%)
  waiting for transfers between devices  70.9 us (21%)
  starting transfers between devices  38.1 us (11%)
  other arithmetic  24.9 us (7%)
  matrix products  17.2 us (5%)
  between operations  14.3 us (4%)
    psum x1, blocking collectives, body(): summed = lax.psum(partial_grad, ('dp', 'ctx'))  93.2 us
    slice x5, local copies, waits for them, and re-layouts, body(): padded[:, k:k + 2 * tok_rows:2, :].astype(jnp.float32)  72.8 us
    all_gather x1, waiting for transfers between devices, body(): value_piece = lax.all_gather(values, 'ctx', axis=1, tiled=True)  29 us
    ppermute x2, waiting for transfers between devices, padded_2(): lax.ppermute(head, axis, [((i + 1) % count, i) for i in range(ends)])  16.2 us
    all_to_all x1, starting transfers between devices, body(): lax.all_to_all(rc_state, 'ctx', split_axis=2, concat_axis=0, tiled=True)  13.8 us
    all_to_all x1, waiting for transfers between devices, body(): lax.all_to_all(rc_state, 'ctx', split_axis=2, concat_axis=0, tiled=True)  12.8 us
    ppermute x2, starting transfers between devices, padded_2(): lax.ppermute(tail, axis, [(i, (i + 1) % count) for i in range(ends)])  11.7 us
    ppermute x2, waiting for transfers between devices, padded_2(): lax.ppermute(tail, axis, [(i, (i + 1) % count) for i in range(ends)])  11.6 us
  transfers between devices with their start and end apart: 8, of which 5 were waited for; matrix products, arithmetic and copies ran while one was open for 32% of the time, Pallas kernels for 0%

commit v1 on v0

--- a/solution.py
+++ b/solution.py
@@ -66,7 +66,9 @@
         .astype(jnp.bfloat16)
     )
     partial_grad = jnp.stack([jnp.sum(grad * taps[k], axis=(0, 1)) for k in range(KW)])
-    summed = lax.psum(partial_grad, ("dp", "ctx"))
+    summed = partial_grad
+    for s in ("ctx", "dp"):
+        summed = lax.psum(summed, s)
     scale = 1.0 / math.sqrt(lax.axis_size("dp") * tok_rows * ctx_count)
     return (d_fine, summed * scale)
 

time: 342 us -> 452 us (1.32)
  blocking collectives: 93.2 us -> 205 us
    psum x1 -> x2, blocking collectives: 93.2 us -> 205 us  [body(): summed = lax.psum(summed, s)]
    ppermute x2, waiting for transfers between devices: 11.6 us -> 6.55 us  [padded_2(): lax.ppermute(tail, axis, [(i, (i + 1) % count) for i in range(ends)])]
  transfers between devices with their start and end apart: 8 -> 8, of which waited for: 5 -> 5; matrix products, arithmetic and copies ran while one was open for 32% -> 24% of each run, Pallas kernels for 0% -> 0%
where the time goes in v1:
time: 452 us; the launch traced here: 451 us
  blocking collectives  205 us (45%)
  local copies, waits for them, and re-layouts  82.9 us (18%)
  waiting for transfers between devices  66.5 us (15%)
  starting transfers between devices  40.3 us (9%)
  other arithmetic  24.9 us (6%)
  matrix products  17.2 us (4%)
  between operations  14.3 us (3%)
    psum x2, blocking collectives, body(): summed = lax.psum(summed, s)  205 us
    slice x5, local copies, waits for them, and re-layouts, body(): padded[:, k:k + 2 * tok_rows:2, :].astype(jnp.float32)  72.8 us
    all_gather x1, waiting for transfers between devices, body(): value_piece = lax.all_gather(values, 'ctx', axis=1, tiled=True)  29 us
    ppermute x2, waiting for transfers between devices, padded_2(): lax.ppermute(head, axis, [((i + 1) % count, i) for i in range(ends)])  16.7 us
    ppermute x2, starting transfers between devices, padded_2(): lax.ppermute(tail, axis, [(i, (i + 1) % count) for i in range(ends)])  13.9 us
    all_to_all x1, starting transfers between devices, body(): lax.all_to_all(rc_state, 'ctx', split_axis=2, concat_axis=0, tiled=True)  13.8 us
    all_to_all x1, waiting for transfers between devices, body(): lax.all_to_all(rc_state, 'ctx', split_axis=2, concat_axis=0, tiled=True)  12.8 us
    dot_general x1, matrix products, body(): jnp.einsum('qhd,kd->qhk', q_heads, key_piece[0], preferred_element_type=j...  9.28 us
  transfers between devices with their start and end apart: 8, of which 5 were waited for; matrix products, arithmetic and copies ran while one was open for 24% of the time, Pallas kernels for 0%

profile of v1, /device:TPU:184, one launch (start us, length us, event | category | flops | bytes accessed | tf_op | source)
XLA Modules:
  0.0 451.0 jit_solution(5041187814327625734)
XLA Ops:
  7.2 0.0 all-gather.3.cloned.1.call-start
  7.2 0.7 all-gather.3.cloned.1.call-update
  7.9 2.2 copy.29
  10.1 0.5 broadcast.15
  10.6 8.8 %reduce.10 = bf16[1536,128]{1,0:T(8,128)(2,1)S(1)} reduce(bf16[1536,1,128]{2,1,0:T(2,128)(2,1)S(1)} %bitcast.34, bf16[]{:T(256)} %broadcast.15), dimensions={1}, to_apply=%bitcast.29.reduce_sub_computation | reduce | bytes 786434
  19.4 0.8 reshape.84
  20.2 13.8 %all-to-all-start = ((bf16[32,2,3072]{2,1,0:T(2,128)(2,1)}), bf16[32,2,3072]{2,1,0:T(2,128)(2,1)S(1)}, u32[]{:S(2)}, u32[]{:S(2)}) async-start(bf16[32,2,3072]{2,1,0:T(2,128)(2,1)} %reshape.84), calls=%async_computation | async-start | bytes 786432 | tf_op jit(solution)/shard_map/all_to_all | solution.py:52
  34.0 0.0 all-gather.5.cloned.1.call-start
  34.1 0.7 all-gather.5.cloned.1.call-update
  34.8 12.8 %all-to-all-done = bf16[32,2,3072]{2,1,0:T(2,128)(2,1)S(1)} async-done(((bf16[32,2,3072]{2,1,0:T(2,128)(2,1)}), bf16[32,2,3072]{2,1,0:T(2,128)(2,1)S(1)}, u32[]{:S(2)}, u32[]{:S(2)}) %all-to-all-start) | async-done | bytes 393248 | tf_op jit(solution)/shard_map/all_to_all | solution.py:52
  47.6 0.3 reshape.85
  47.9 0.1 copy.31
  48.0 0.8 rev.6
  48.7 8.5 %all-to-all-start.1 = ((bf16[32,128,48]{1,2,0:T(8,128)(2,1)}), bf16[32,128,48]{1,2,0:T(8,128)(2,1)S(1)}, u32[]{:S(2)}, u32[]{:S(2)}) async-start(bf16[32,128,48]{1,2,0:T(8,128)(2,1)} %rev.6), calls=%async_computation.1 | async-start | bytes 786432 | tf_op jit(solution)/shard_map/all_to_all | solution.py:54
  57.3 0.3 copy.24
  57.5 5.5 %collective-permute-start = (bf16[1,2,1536]{1,2,0:T(8,128)(2,1)S(1)}, bf16[1,2,1536]{1,2,0:T(8,128)(2,1)}, u32[]{:S(2)}, u32[]{:S(2)}) collective-permute-start(bf16[1,2,1536]{1,2,0:T(8,128)(2,1)S(1)} %copy.24), channel_id=1, source_target_pairs={{0,1},{1,2},{2,3},{3,4},{4,5},{5,6},{6,7},{7,8},{8,9},{9,10},{10,1... | collective-permute-start | bytes 18440 | tf_op jit(solution)/shard_map/ppermute | solution.py:19
  63.0 0.3 copy.25
  63.3 2.1 collective-permute-start.1
  65.4 0.1 slice_reduce_fusion.4
  65.5 0.3 copy.26
  65.8 1.0 copy.32
  66.8 14.4 %slice.65 = bf16[1,128,1536]{1,2,0:T(8,128)(2,1)S(1)} slice(bf16[1,256,1536]{1,2,0:T(8,128)(2,1)S(1)} %copy.26), slice={[0:1:1], [0:256:2], [0:1536:1]} | slice | bytes 786432 | tf_op jit(solution)/shard_map/slice | solution.py:48
  81.2 5.9 %collective-permute-done.1 = bf16[1,2,1536]{1,2,0:T(8,128)(2,1)} collective-permute-done((bf16[1,2,1536]{1,2,0:T(8,128)(2,1)S(1)}, bf16[1,2,1536]{1,2,0:T(8,128)(2,1)}, u32[]{:S(2)}, u32[]{:S(2)}) %collective-permute-start.1) | collective-permute-done | bytes 6176 | tf_op jit(solution)/shard_map/ppermute | solution.py:21
  87.1 1.8 pad_maximum_fusion
  88.9 14.4 %slice.61 = bf16[1,128,1536]{1,2,0:T(8,128)(2,1)S(1)} slice(bf16[1,260,1536]{1,2,0:T(8,128)(2,1)S(1)} %pad_maximum_fusion), slice={[0:1:1], [0:256:2], [0:1536:1]} | slice | bytes 786432 | tf_op jit(solution)/shard_map/slice | solution.py:48
  103.3 14.4 %slice.63 = bf16[1,128,1536]{1,2,0:T(8,128)(2,1)S(1)} slice(bf16[1,260,1536]{1,2,0:T(8,128)(2,1)S(1)} %pad_maximum_fusion), slice={[0:1:1], [1:257:2], [0:1536:1]} | slice | bytes 786432 | tf_op jit(solution)/shard_map/slice | solution.py:48
  117.7 14.7 %slice.67 = bf16[1,128,1536]{1,2,0:T(8,128)(2,1)S(1)} slice(bf16[1,260,1536]{1,2,0:T(8,128)(2,1)S(1)} %pad_maximum_fusion), slice={[0:1:1], [3:259:2], [0:1536:1]} | slice | bytes 786432 | tf_op jit(solution)/shard_map/slice | solution.py:48
  132.4 15.0 %slice.69 = bf16[1,128,1536]{1,2,0:T(8,128)(2,1)} slice(bf16[1,260,1536]{1,2,0:T(8,128)(2,1)S(1)} %pad_maximum_fusion), slice={[0:1:1], [4:260:2], [0:1536:1]} | slice | bytes 786432 | tf_op jit(solution)/shard_map/slice | solution.py:48
  147.4 1.3 rev.7
  148.8 9.3 %multiply_reduce_fusion = (f32[128,8]{0,1:T(8,128)S(1)}, f32[128,8,4096]{2,0,1:T(8,128)}) fusion(bf16[1,4096,128]{2,1,0:T(8,128)(2,1)} %all-gather.3.cloned.1.call-done, bf16[128,8,128]{2,1,0:T(8,128)(2,1)S(1)} %bitcast.36), kind=kOutput, calls=%fused_computation.1 | convolution fusion | flops 1082129408 | bytes 18092032 | tf_op jit(solution)/shard_map/qhd,kd->qhk/dot_general | solution.py:37
  158.0 8.6 %fusion = f32[128,8]{0,1:T(8,128)S(1)} fusion(f32[128,8,4096]{2,0,1:T(8,128)} %get-tuple-element.20, f32[128,8]{0,1:T(8,128)S(1)} %broadcast_maximum_fusion), kind=kLoop, calls=%fused_computation.2 | loop fusion | flops 12581888 | bytes 16785408 | tf_op jit(solution)/shard_map/reduce_sum | solution.py:42
  166.7 29.0 %all-gather.5.cloned.1.call-done = bf16[1,4096,192]{1,2,0:T(8,128)(2,1)} async-done(((bf16[1,128,192]{1,2,0:T(8,128)(2,1)}), bf16[1,4096,192]{1,2,0:T(8,128)(2,1)}) %all-gather.5.cloned.1.call-update) | async-done | bytes 1572880 | tf_op jit(solution)/shard_map/all_gather | solution.py:36
  195.6 8.0 %fusion.7 = f32[128,8,192]{0,2,1:T(8,128)S(1)} fusion(bf16[1,4096,192]{1,2,0:T(8,128)(2,1)} %all-gather.5.cloned.1.call-done, f32[128,8,4096]{2,0,1:T(8,128)} %get-tuple-element.20, f32[128,8]{0,1:T(8,128)S(1)} %broadcast_maximum_fusion, f32[128,8]{0,1:T(8,128)S(1)} %fusion), kind=kOutput, calls=%fused_computation.19 | convolution fusion | flops 1623392256 | bytes 19144704 | tf_op jit(solution)/shard_map/qhk,kv->qhv/dot_general | solution.py:43
  203.6 2.7 fusion.22
  206.4 0.1 stack.38
  206.5 152.0 %psum.14 = f32[5,1536]{1,0:T(8,128)S(1)} all-reduce(f32[5,1536]{1,0:T(8,128)S(1)} %stack.38), channel_id=1, replica_groups=mesh['dp'=16,'ctx'=32] {'ctx'}, use_global_device_ids=true, to_apply=%region_7.0 | all-reduce | flops 7680 | bytes 61440 | tf_op jit(solution)/shard_map/psum | solution.py:71
  358.5 53.0 %psum.15 = f32[5,1536]{1,0:T(8,128)S(1)} all-reduce(f32[5,1536]{1,0:T(8,128)S(1)} %psum.14), channel_id=1, replica_groups=mesh['dp'=16,'ctx'=32] {'dp'}, use_global_device_ids=true, to_apply=%region_8.0 | all-reduce | flops 7680 | bytes 61440 | tf_op jit(solution)/shard_map/psum | solution.py:71
  411.5 0.2 fusion.31
  411.6 8.4 %collective-permute-start.2 = (bf16[1,1,1536]{1,2,0:T(8,128)(2,1)S(1)}, bf16[1,1,1536]{1,2,0:T(8,128)(2,1)S(1)}, u32[]{:S(2)}, u32[]{:S(2)}) collective-permute-start(bf16[1,1,1536]{1,2,0:T(8,128)(2,1)S(1)} %get-tuple-element.17), channel_id=1, source_target_pairs={{0,1},{1,2},{2,3},{3,4},{4,5},{5,6},{6,7},{7,8},{8,9},{9,10},{10,1... | collective-permute-start | bytes 9224 | tf_op jit(solution)/shard_map/ppermute | solution.py:19
  420.1 1.9 collective-permute-start.3
  422.0 0.6 broadcast_multiply_fusion
  422.6 6.5 %collective-permute-done.2 = bf16[1,1,1536]{1,2,0:T(8,128)(2,1)S(1)} collective-permute-done((bf16[1,1,1536]{1,2,0:T(8,128)(2,1)S(1)}, bf16[1,1,1536]{1,2,0:T(8,128)(2,1)S(1)}, u32[]{:S(2)}, u32[]{:S(2)}) %collective-permute-start.2) | collective-permute-done | bytes 3104 | tf_op jit(solution)/shard_map/ppermute | solution.py:19
  429.2 10.9 %collective-permute-done.3 = bf16[1,1,1536]{1,2,0:T(8,128)(2,1)S(1)} collective-permute-done((bf16[1,1,1536]{1,2,0:T(8,128)(2,1)S(1)}, bf16[1,1,1536]{1,2,0:T(8,128)(2,1)S(1)}, u32[]{:S(2)}, u32[]{:S(2)}) %collective-permute-start.3) | collective-permute-done | bytes 3104 | tf_op jit(solution)/shard_map/ppermute | solution.py:21
  440.0 0.4 maximum_convert_fusion
  440.5 1.7 fusion.26
  442.2 0.1 pad_maximum_fusion.1
  442.3 0.8 copy.30
  443.0 1.2 convert_element_type.56
  (16 shorter events, 0.1 us)
Async XLA Ops:
  7.2 141.6 %all-gather.3.cloned.1.call-start = ((), (), s32[]{:S(2)}) async-start(), calls=%async_computation.2 | async-start | bytes 1081344 | tf_op jit(solution)/shard_map/all_gather | solution.py:35
  20.2 37.0 %copy-start.1 = (bf16[1,256,1536]{2,1,0:T(8,128)(2,1)S(1)}, bf16[1,256,1536]{2,1,0:T(8,128)(2,1)}, u32[]{:S(2)}) copy-start(bf16[1,256,1536]{2,1,0:T(8,128)(2,1)} %param.9) | copy-start | bytes 2359300
  20.2 27.4 %all-to-all-start = ((bf16[32,2,3072]{2,1,0:T(2,128)(2,1)}), bf16[32,2,3072]{2,1,0:T(2,128)(2,1)S(1)}, u32[]{:S(2)}, u32[]{:S(2)}) async-start(bf16[32,2,3072]{2,1,0:T(2,128)(2,1)} %reshape.84), calls=%async_computation | async-start | bytes 786432 | tf_op jit(solution)/shard_map/all_to_all | solution.py:52
  34.0 161.6 %all-gather.5.cloned.1.call-start = ((), (), s32[]{:S(2)}) async-start(), calls=%async_computation.3 | async-start | bytes 1622016 | tf_op jit(solution)/shard_map/all_gather | solution.py:36
  34.8 30.6 %copy-start.2 = (f32[5,1536]{1,0:T(8,128)S(1)}, f32[5,1536]{1,0:T(8,128)}, u32[]{:S(2)}) copy-start(f32[5,1536]{1,0:T(8,128)} %param.11) | copy-start | bytes 92164
  48.7 98.6 %all-to-all-start.1 = ((bf16[32,128,48]{1,2,0:T(8,128)(2,1)}), bf16[32,128,48]{1,2,0:T(8,128)(2,1)S(1)}, u32[]{:S(2)}, u32[]{:S(2)}) async-start(bf16[32,128,48]{1,2,0:T(8,128)(2,1)} %rev.6), calls=%async_computation.1 | async-start | bytes 786432 | tf_op jit(solution)/shard_map/all_to_all | solution.py:54
  57.5 23.6 %collective-permute-start = (bf16[1,2,1536]{1,2,0:T(8,128)(2,1)S(1)}, bf16[1,2,1536]{1,2,0:T(8,128)(2,1)}, u32[]{:S(2)}, u32[]{:S(2)}) collective-permute-start(bf16[1,2,1536]{1,2,0:T(8,128)(2,1)S(1)} %copy.24), channel_id=1, source_target_pairs={{0,1},{1,2},{2,3},{3,4},{4,5},{5,6},{6,7},{7,8},{8,9},{9,10},{10,1... | collective-permute-start | bytes 18440 | tf_op jit(solution)/shard_map/ppermute | solution.py:19
  63.3 23.8 %collective-permute-start.1 = (bf16[1,2,1536]{1,2,0:T(8,128)(2,1)S(1)}, bf16[1,2,1536]{1,2,0:T(8,128)(2,1)}, u32[]{:S(2)}, u32[]{:S(2)}) collective-permute-start(bf16[1,2,1536]{1,2,0:T(8,128)(2,1)S(1)} %copy.25), channel_id=1, source_target_pairs={{1,0},{2,1},{3,2},{4,3},{5,4},{6,5},{7,6},{8,7},{9,8},{10,9},{11,1... | collective-permute-start | bytes 18440 | tf_op jit(solution)/shard_map/ppermute | solution.py:21
  166.7 36.9 %copy-start = (bf16[1,128,1536]{1,2,0:T(8,128)(2,1)S(1)}, bf16[1,128,1536]{1,2,0:T(8,128)(2,1)}, u32[]{:S(2)}) copy-start(bf16[1,128,1536]{1,2,0:T(8,128)(2,1)} %slice.69) | copy-start | bytes 1179652
  411.6 17.6 %collective-permute-start.2 = (bf16[1,1,1536]{1,2,0:T(8,128)(2,1)S(1)}, bf16[1,1,1536]{1,2,0:T(8,128)(2,1)S(1)}, u32[]{:S(2)}, u32[]{:S(2)}) collective-permute-start(bf16[1,1,1536]{1,2,0:T(8,128)(2,1)S(1)} %get-tuple-element.17), channel_id=1, source_target_pairs={{0,1},{1,2},{2,3},{3,4},{4,5},{5,6},{6,7},{7,8},{8,9},{9,10},{10,1... | collective-permute-start | bytes 9224 | tf_op jit(solution)/shard_map/ppermute | solution.py:19
  420.1 20.0 %collective-permute-start.3 = (bf16[1,1,1536]{1,2,0:T(8,128)(2,1)S(1)}, bf16[1,1,1536]{1,2,0:T(8,128)(2,1)S(1)}, u32[]{:S(2)}, u32[]{:S(2)}) collective-permute-start(bf16[1,1,1536]{1,2,0:T(8,128)(2,1)S(1)} %get-tuple-element.18), channel_id=1, source_target_pairs={{1,0},{2,1},{3,2},{4,3},{5,4},{6,5},{7,6},{8,7},{9,8},{10,9},{11,1... | collective-permute-start | bytes 9224 | tf_op jit(solution)/shard_map/ppermute | solution.py:21
Sparse Core Ops, SparseCore 0:
  11.2 102.2 all-gather.2
  116.5 79.0 all-gather.4
